TPU v7x, 32 devices: a whole 2x2x4 slice. The times are simulated.
32 devices in a mesh: gx: 8 (over z, core), gy: 4 (over y, x).
Axes of the slice: x: 2, y: 2, z: 4, core: 2. Of those that a mesh axis runs over, the one named last changes fastest.
Arguments:
- u_velocity: float32 [128, 128, 512], P('gx', 'gy'), may hold values from -5 to 5
- v_velocity: float32 [128, 128, 512], P('gx', 'gy'), may hold values from -5 to 5
- w_velocity: float32 [128, 128, 512], P('gx', 'gy'), may hold values from -5 to 5
- viscosity: float32 [128, 128, 512], P('gx', 'gy'), may hold values from 0.5 to 2
- cell_width: float32 [128], P('gx'), may hold values from 0.003 to 0.008
Outputs:
- u_next: float32 [128, 128, 512], P('gx', 'gy')
- v_next: float32 [128, 128, 512], P('gx', 'gy')
- w_next: float32 [128, 128, 512], P('gx', 'gy')
All inputs are finite; a program needn't handle non-finite values.
Results may differ from a plain program's by a relative error of at most 0.0002.
Values sent between devices are 32-bit elements; how exact they have to be, the bound alone decides.
A program may use at most 128 MiB of HBM per device.

v0:
```python
import jax
import jax.numpy as jnp
from jax import lax
from jax.sharding import PartitionSpec as P

time_step = 0.0125
lateral_step = 0.5
vertical_step = 0.5


def padded_2(block, sides, width):
    for axis, dim in sides:
        count = lax.axis_size(axis)
        forward = [(i, i + 1) for i in range(count - 1)]
        backward = [(target, source) for source, target in forward]
        low = lax.ppermute(
            lax.slice_in_dim(block, block.shape[dim] - width, None, axis=dim), axis, forward
        )
        high = lax.ppermute(lax.slice_in_dim(block, 0, width, axis=dim), axis, backward)
        block = jnp.concatenate([low, block, high], axis=dim)
    return block


def from_behind(block, axis, distance):
    devices = range(lax.axis_size(axis))
    route = [(i - distance, i) for i in devices if i - distance in devices]
    return lax.ppermute(block, axis, route)


def thomas(sub_coef, diag_coef, sup_coef, right_side):

    def forward(state_pair, row_data):
        ratio_prev, value_prev = state_pair
        sub_row, diag_row, sup_row, side_row = row_data
        denom = diag_row - sub_row * ratio_prev
        ratio_now = sup_row / denom
        value_now = (side_row - sub_row[None] * value_prev) / denom[None]
        return ((ratio_now, value_now), (ratio_now, value_now))

    start = (jnp.zeros_like(diag_coef[0]), jnp.zeros_like(right_side[0]))
    _, (ratios, values) = lax.scan(forward, start, (sub_coef, diag_coef, sup_coef, right_side))

    def backward(after, row_data):
        ratio_row, value_row = row_data
        result = value_row - ratio_row[None] * after
        return (result, result)

    _, solved = lax.scan(backward, jnp.zeros_like(right_side[0]), (ratios, values), reverse=True)
    return solved


def explicit_terms(padded, widths):
    u_all, v_all, w_all, viscous = (padded[0], padded[1], padded[2], padded[3])
    rows_x = padded.shape[1] - 2
    rows_y = padded.shape[2] - 2
    rows_z = padded.shape[3] - 2

    def interior(values_in, shift_x, shift_y, shift_z):
        return values_in[
            1 + shift_x : 1 + shift_x + rows_x,
            1 + shift_y : 1 + shift_y + rows_y,
            1 + shift_z : 1 + shift_z + rows_z,
        ]

    width_mid = widths[1:-1][:, None, None]
    width_low = widths[:-2][:, None, None]
    width_high = widths[2:][:, None, None]
    centre_span = 0.5 * width_low + width_mid + 0.5 * width_high
    visc_mid = interior(viscous, 0, 0, 0)
    below_coef = (
        time_step
        * 0.5
        * (visc_mid + interior(viscous, -1, 0, 0))
        / (width_mid * 0.5 * (width_low + width_mid))
    )
    above_coef = (
        time_step
        * 0.5
        * (visc_mid + interior(viscous, 1, 0, 0))
        / (width_mid * 0.5 * (width_mid + width_high))
    )
    half_y = 0.5 / lateral_step
    half_z = 0.5 / vertical_step
    flux_vx = viscous[1:-1] * (v_all[2:] - v_all[:-2]) / centre_span
    flux_wx = viscous[1:-1] * (w_all[2:] - w_all[:-2]) / centre_span
    cross_u = (flux_vx[:, 2:, 1:-1] - flux_vx[:, :-2, 1:-1]) * half_y + (
        flux_wx[:, 1:-1, 2:] - flux_wx[:, 1:-1, :-2]
    ) * half_z
    flux_uy = viscous[:, 1:-1] * (u_all[:, 2:] - u_all[:, :-2]) * half_y
    flux_wy = viscous[:, 1:-1] * (w_all[:, 2:] - w_all[:, :-2]) * half_y
    cross_v = (flux_uy[2:, :, 1:-1] - flux_uy[:-2, :, 1:-1]) / centre_span + (
        flux_wy[1:-1, :, 2:] - flux_wy[1:-1, :, :-2]
    ) * half_z
    flux_uz = viscous[:, :, 1:-1] * (u_all[:, :, 2:] - u_all[:, :, :-2]) * half_z
    flux_vz = viscous[:, :, 1:-1] * (v_all[:, :, 2:] - v_all[:, :, :-2]) * half_z
    cross_w = (flux_uz[2:, 1:-1] - flux_uz[:-2, 1:-1]) / centre_span + (
        flux_vz[1:-1, 2:] - flux_vz[1:-1, :-2]
    ) * half_y
    u_mid = interior(u_all, 0, 0, 0)
    v_mid = interior(v_all, 0, 0, 0)
    w_mid = interior(w_all, 0, 0, 0)
    sides = []
    for values_in, cross_term in ((u_all, cross_u), (v_all, cross_v), (w_all, cross_w)):
        advect = -(
            u_mid * ((interior(values_in, 1, 0, 0) - interior(values_in, -1, 0, 0)) / centre_span)
            + v_mid
            * (
                (interior(values_in, 0, 1, 0) - interior(values_in, 0, -1, 0))
                * (0.5 / lateral_step)
            )
            + w_mid
            * (
                (interior(values_in, 0, 0, 1) - interior(values_in, 0, 0, -1))
                * (0.5 / vertical_step)
            )
        )
        centre_value = interior(values_in, 0, 0, 0)
        total = jnp.zeros_like(centre_value)
        for offset_y, offset_z, spacing in ((1, 0, lateral_step), (0, 1, vertical_step)):
            high_visc = 0.5 * (visc_mid + interior(viscous, 0, offset_y, offset_z))
            low_visc = 0.5 * (visc_mid + interior(viscous, 0, -offset_y, -offset_z))
            high_value = interior(values_in, 0, offset_y, offset_z)
            low_value = interior(values_in, 0, -offset_y, -offset_z)
            total = total + (
                high_visc * (high_value - centre_value) - low_visc * (centre_value - low_value)
            ) / (spacing * spacing)
        sides.append(interior(values_in, 0, 0, 0) + time_step * (advect + total + cross_term))
    return (jnp.stack(sides, axis=1), below_coef, above_coef)


def per_device(u_velocity, v_velocity, w_velocity, viscosity, cell_width):
    stacked = jnp.stack([u_velocity, v_velocity, w_velocity, viscosity])
    haloed = padded_2(stacked, (("gx", 1), ("gy", 2)), 1)
    padded = jnp.pad(haloed, ((0, 0), (0, 0), (0, 0), (1, 1)))
    widths = padded_2(cell_width, (("gx", 0),), 1)
    right_side, below_coef, above_coef = explicit_terms(padded, widths)
    diagonal = 1.0 + below_coef + above_coef
    rows_x = right_side.shape[0]
    inside = rows_x - 1
    row_index = lax.broadcasted_iota(jnp.int32, (inside, 1, 1), 0)
    left_unit = jnp.where(row_index == 0, below_coef[:inside], 0.0)
    right_unit = jnp.where(row_index == inside - 1, above_coef[:inside], 0.0)
    columns = jnp.concatenate(
        [right_side[:inside], left_unit[:, None], right_unit[:, None]], axis=1
    )
    solved = thomas(-below_coef[:inside], diagonal[:inside], -above_coef[:inside], columns)
    following = from_behind(solved[0], "gx", -1)
    last_below = below_coef[inside]
    last_above = above_coef[inside]
    before_row = solved[inside - 1]
    reduced_sub = -last_below * before_row[3]
    reduced_diag = diagonal[inside] - last_below * before_row[4] - last_above * following[3]
    reduced_sup = -last_above * following[4]
    reduced_side = (
        right_side[inside] + last_below[None] * before_row[:3] + last_above[None] * following[:3]
    )
    reduced = jnp.concatenate(
        [reduced_sub[None], reduced_diag[None], reduced_sup[None], reduced_side], axis=0
    )
    span_y = reduced.shape[1]
    span_z = reduced.shape[2]
    groups = lax.axis_size("gx")
    line_rows = reduced.reshape(1, 6, groups, span_y * span_z // groups)
    received = lax.all_to_all(line_rows, "gx", split_axis=2, concat_axis=0, tiled=True)
    answers = thomas(received[:, 0], received[:, 1], received[:, 2], received[:, 3:6])
    shifted = jnp.concatenate([jnp.zeros_like(answers[:1]), answers[:-1]], axis=0)
    paired = jnp.concatenate([shifted, answers], axis=1)
    returned = lax.all_to_all(paired, "gx", split_axis=0, concat_axis=2, tiled=True)
    returned = returned.reshape(6, span_y, span_z)
    left_value = returned[:3]
    own_value = returned[3:]
    inner_part = (
        solved[:, :3] + solved[:, 3:4] * left_value[None] + solved[:, 4:5] * own_value[None]
    )
    complete = jnp.concatenate([inner_part, own_value[None]], axis=0)
    return (complete[:, 0], complete[:, 1], complete[:, 2])


def solution(mesh):
    return jax.shard_map(
        per_device,
        mesh=mesh,
        in_specs=(
            P("gx", "gy", None),
            P("gx", "gy", None),
            P("gx", "gy", None),
            P("gx", "gy", None),
            P("gx"),
        ),
        out_specs=(P("gx", "gy", None), P("gx", "gy", None), P("gx", "gy", None)),
        check_vma=False,
    )
```

profile of v0, /device:TPU:0, one launch (start us, length us, event | category | flops | bytes accessed | tf_op | source)
XLA Modules:
  0.0 218.7 jit_solution(4723233457754301835)
XLA Ops:
  0.7 2.0 pad_maximum_fusion.8
  2.7 3.1 %collective-permute-start = (f32[4,1,32,512]{3,2,1,0:T(8,128)}, f32[4,1,32,512]{3,2,1,0:T(8,128)}, u32[]{:S(2)}, u32[]{:S(2)}) collective-permute-start(f32[4,1,32,512]{3,2,1,0:T(8,128)} %get-tuple-element.520), channel_id=1, source_target_pairs={{0,4},{4,8},{8,12},{12,16},{16,20},{20,24},{24,28},{1,5},{5,9},{9,... | collective-permute-start | bytes 786440 | tf_op jit(solution)/shard_map/ppermute | solution.py:16
  9.0 5.7 %collective-permute-start.5 = (f32[1]{0:T(128)}, f32[1]{0:T(128)}, u32[]{:S(2)}, u32[]{:S(2)}) collective-permute-start(f32[1]{0:T(128)} %get-tuple-element.547), channel_id=1, source_target_pairs={{0,4},{4,8},{8,12},{12,16},{16,20},{20,24},{24,28},{1,5},{5,9},{9,... | collective-permute-start | bytes 20 | tf_op jit(solution)/shard_map/ppermute | solution.py:16
  17.9 3.4 %collective-permute-start.2 = (f32[4,18,1,512]{3,2,1,0:T(1,128)S(1)}, f32[4,18,1,512]{3,2,1,0:T(1,128)S(1)}, u32[]{:S(2)}, u32[]{:S(2)}) collective-permute-start(f32[4,18,1,512]{3,2,1,0:T(1,128)S(1)} %get-tuple-element.518), channel_id=1, source_target_pairs={{0,1},{1,2},{2,3},{4,5},{5,6},{6,7},{8,9},{9,10},{10,11},{12,13},{... | collective-permute-start | bytes 442376 | tf_op jit(solution)/shard_map/ppermute | solution.py:16
  22.7 2.1 collective-permute-done.2
  24.8 5.2 %collective-permute-done.3 = f32[4,18,1,512]{3,2,1,0:T(1,128)S(1)} collective-permute-done((f32[4,18,1,512]{3,2,1,0:T(1,128)S(1)}, f32[4,18,1,512]{3,2,1,0:T(1,128)S(1)}, u32[]{:S(2)}, u32[]{:S(2)}) %collective-permute-start.3) | collective-permute-done | bytes 147488 | tf_op jit(solution)/shard_map/ppermute | solution.py:19
  30.0 2.5 %pad_maximum_fusion = f32[4,18,34,512]{3,2,1,0:T(8,128)S(1)} fusion(f32[4,18,1,512]{3,2,1,0:T(1,128)S(1)} %collective-permute-done.3, f32[4,1,32,512]{3,2,1,0:T(8,128)} %collective-permute-done.1, f32[1,16,32,512]{3,2,1,0:T(8,128)S(1)} %bitcast.182, f32[1,16,32,512]{3,2,1,0:T(8,128)S(1)} %bitcast.185, f32[1,16,32,512]{3,2,1,0:T(8,128)S(1)} %bitcast.188, ...), kind=kLoop, calls=%fused_computation.38 | loop fusion | flops 8773632 | bytes 10027008 | tf_op jit(solution)/shard_map/concatenate | solution.py:20
  34.5 2.6 %fusion.16 = (f32[16,34,514]{2,1,0:T(8,128)S(1)}, f32[16,34,514]{2,1,0:T(8,128)S(1)}) fusion(f32[4,18,34,512]{3,2,1,0:T(8,128)S(1)} %pad_maximum_fusion, f32[16]{0:T(128)S(1)} %get-tuple-element.541), kind=kLoop, calls=%fused_computation.54 | loop fusion | flops 1677696 | bytes 7250496 | tf_op jit(solution)/shard_map/div | solution.py:84
  38.9 5.0 %fusion.58 = f32[16,1,32,512]{3,2,1,0:T(8,128)S(1)} fusion(f32[16,34,514]{2,1,0:T(8,128)S(1)} %get-tuple-element.511, f32[16,34,514]{2,1,0:T(8,128)S(1)} %get-tuple-element.510, f32[18,34,514]{2,1,0:T(8,128)S(1)} %get-tuple-element.513, f32[18,34,514]{2,1,0:T(8,128)S(1)} %get-tuple-element.512, f32[18,34,514]{2,1,0:T(8,128)S(1)} %get-tuple-element.514, ...), kind=kLoop, calls=%fused_computation.109 | loop fusion | flops 9699328 | bytes 19923008 | tf_op jit(solution)/shard_map/stack | solution.py:128
  44.0 4.8 %fusion.46 = f32[16,1,32,512]{3,2,1,0:T(8,128)S(1)} fusion(f32[18,32,514]{2,1,0:T(8,128)S(1)} %get-tuple-element.526, f32[18,32,514]{2,1,0:T(8,128)S(1)} %get-tuple-element.525, f32[18,34,514]{2,1,0:T(8,128)S(1)} %get-tuple-element.514, f32[18,34,514]{2,1,0:T(8,128)S(1)} %get-tuple-element.512, f32[18,34,514]{2,1,0:T(8,128)S(1)} %get-tuple-element.513, ...), kind=kLoop, calls=%fused_computation.94 | loop fusion | flops 9961472 | bytes 19923008 | tf_op jit(solution)/shard_map/stack | solution.py:128
  48.8 4.3 %fusion.34 = f32[16,1,32,512]{3,2,1,0:T(8,128)S(1)} fusion(f32[18,34,512]{2,1,0:T(8,128)S(1)} %get-tuple-element.528, f32[18,34,512]{2,1,0:T(8,128)S(1)} %get-tuple-element.527, f32[18,34,514]{2,1,0:T(8,128)S(1)} %get-tuple-element.512, f32[18,34,514]{2,1,0:T(8,128)S(1)} %get-tuple-element.514, f32[18,34,514]{2,1,0:T(8,128)S(1)} %get-tuple-element.513, ...), kind=kLoop, calls=%fused_computation.79 | loop fusion | flops 9961472 | bytes 19923008 | tf_op jit(solution)/shard_map/stack | solution.py:128
  60.0 2.9 %pad_maximum_fusion.1 = f32[15,5,32,512]{3,2,1,0:T(8,128)} fusion(f32[15,1,32,512]{3,2,1,0:T(8,128)S(1)} %get-tuple-element.534, f32[15,1,32,512]{3,2,1,0:T(8,128)S(1)} %get-tuple-element.549, f32[15,3,32,512]{3,2,1,0:T(8,128)S(1)} %slice-done), kind=kLoop, calls=%fused_computation.39 | loop fusion | flops 2457600 | bytes 9830400 | tf_op jit(solution)/shard_map/concatenate | solution.py:143
  62.9 2.9 %broadcast.64.clone = f32[15,5,32,512]{3,2,1,0:T(8,128)} broadcast(f32[]{:T(128)} %constant.129.clone.1), dimensions={} | broadcast | bytes 4915204 | tf_op jit(solution)/shard_map/broadcast.13
  66.9 53.6 %while.68 = (s32[]{:T(128)}, f32[32,512]{1,0:T(8,128)S(1)}, f32[5,32,512]{2,1,0:T(8,128)}, f32[15,32,512]{2,1,0:T(8,128)}, f32[15,5,32,512]{3,2,1,0:T(8,128)}, /...) while((s32[]{:T(128)}, f32[32,512]{1,0:T(8,128)S(1)}, ...), condition=%wide.region_1.2_spmd.clone, body=%wide.region_0.1_spmd.clone.sunk | while | flops 393219 | bytes 1967224 | solution.py:41
  71.9 2.0 bitcast_dynamic-update-slice_fusion.13
  79.1 2.0 bitcast_dynamic-update-slice_fusion.13
  82.6 2.0 bitcast_dynamic-update-slice_fusion.13
  86.2 2.0 bitcast_dynamic-update-slice_fusion.13
  93.4 2.0 bitcast_dynamic-update-slice_fusion.13
  96.9 2.1 bitcast_dynamic-update-slice_fusion.13
  100.5 2.0 bitcast_dynamic-update-slice_fusion.13
  104.1 2.0 bitcast_dynamic-update-slice_fusion.13
  107.7 2.0 bitcast_dynamic-update-slice_fusion.13
  114.9 2.0 bitcast_dynamic-update-slice_fusion.13
  120.5 2.9 %broadcast.64 = f32[15,5,32,512]{3,2,1,0:T(8,128)} broadcast(f32[]{:T(128)} %constant.129.clone.1), dimensions={} | broadcast | bytes 4915204 | tf_op jit(solution)/shard_map/broadcast.13
  123.3 41.1 %while.69 = (s32[]{:T(128)}, f32[5,32,512]{2,1,0:T(8,128)S(1)}, f32[15,5,32,512]{3,2,1,0:T(8,128)}, f32[15,5,32,512]{3,2,1,0:T(8,128)}, f32[15,32,512]{2,1,0:T(8,128)}, /*index=5*/s32[]{:T(128)}, s32[]{:T(128)}, s32[]{:T(128)}) while((s32[]{:T(128)}, f32[5,32,512]{2,1,0:T(8,128)S(1)}, f32[15,5,32,512]{3,2,1,0:T(8,128)}, ...), condition=%wide.region_3.4_spmd.clone, body=%wide.region_2.3_spmd.clone.sunk | while | flops 245764 | bytes 1507443 | solution.py:48
  166.7 2.2 %collective-permute-done.6 = f32[5,32,512]{2,1,0:T(8,128)S(1)} collective-permute-done((f32[5,32,512]{2,1,0:T(8,128)S(1)}, f32[5,32,512]{2,1,0:T(8,128)S(1)}, u32[]{:S(2)}, u32[]{:S(2)}) %collective-permute-start.6) | collective-permute-done | bytes 327712 | tf_op jit(solution)/shard_map/ppermute | solution.py:27
  172.4 9.6 %all-to-all-start = ((f32[1,6,8,2048]{3,0,1,2:T(1,128)}), f32[1,6,8,2048]{3,0,1,2:T(1,128)S(1)}, u32[]{:S(2)}, u32[]{:S(2)}) async-start(f32[1,6,8,2048]{3,0,1,2:T(1,128)} %copy.45), calls=%async_computation | async-start | bytes 786432 | tf_op jit(solution)/shard_map/all_to_all | solution.py:164
  182.0 12.5 %all-to-all-done = f32[1,6,8,2048]{3,0,1,2:T(1,128)S(1)} async-done(((f32[1,6,8,2048]{3,0,1,2:T(1,128)}), f32[1,6,8,2048]{3,0,1,2:T(1,128)S(1)}, u32[]{:S(2)}, u32[]{:S(2)}) %all-to-all-start) | async-done | bytes 393248 | tf_op jit(solution)/shard_map/all_to_all | solution.py:164
  198.0 3.5 %all-to-all-start.1 = ((f32[8,6,1,2048]{3,2,1,0:T(1,128)}), f32[8,6,1,2048]{3,2,1,0:T(1,128)S(1)}, u32[]{:S(2)}, u32[]{:S(2)}) async-start(f32[8,6,1,2048]{3,2,1,0:T(1,128)} %fusion.73), calls=%async_computation.1 | async-start | bytes 786432 | tf_op jit(solution)/shard_map/all_to_all | solution.py:168
  203.2 10.8 %all-to-all-done.1 = f32[8,6,1,2048]{3,2,1,0:T(1,128)S(1)} async-done(((f32[8,6,1,2048]{3,2,1,0:T(1,128)}), f32[8,6,1,2048]{3,2,1,0:T(1,128)S(1)}, u32[]{:S(2)}, u32[]{:S(2)}) %all-to-all-start.1) | async-done | bytes 393248 | tf_op jit(solution)/shard_map/all_to_all | solution.py:168
  214.3 2.6 %fusion.8 = f32[15,3,32,512]{3,2,0,1:T(8,128)S(1)} fusion(f32[3,32,512]{2,1,0:T(8,128)S(1)} %mul.347, f32[15,32,512]{2,1,0:T(8,128)S(1)} %get-tuple-element.517, f32[3,32,512]{2,1,0:T(8,128)S(1)} %mul.342, f32[15,32,512]{2,1,0:T(8,128)S(1)} %get-tuple-element.516, f32[15,5,32,512]{3,2,1,0:T(8,128)} %get-tuple-element.307), kind=kLoop, calls=%fused_computation.46 | loop fusion | flops 2949120 | bytes 8257536 | tf_op jit(solution)/shard_map/add | solution.py:173
  (165 shorter events, 108.2 us)
Async XLA Ops:
  0.6 15.8 %copy-start.3 = (f32[16,32,512]{2,1,0:T(8,128)S(1)}, f32[16,32,512]{2,1,0:T(8,128)}, u32[]{:S(2)}) copy-start(f32[16,32,512]{2,1,0:T(8,128)} %param.14) | copy-start | bytes 3145732
  0.6 15.8 %copy-start.2 = (f32[16,32,512]{2,1,0:T(8,128)S(1)}, f32[16,32,512]{2,1,0:T(8,128)}, u32[]{:S(2)}) copy-start(f32[16,32,512]{2,1,0:T(8,128)} %param.15) | copy-start | bytes 3145732
  0.7 15.8 %copy-start.1 = (f32[16,32,512]{2,1,0:T(8,128)S(1)}, f32[16,32,512]{2,1,0:T(8,128)}, u32[]{:S(2)}) copy-start(f32[16,32,512]{2,1,0:T(8,128)} %param.16) | copy-start | bytes 3145732
  0.7 6.4 %copy-start.8 = (f32[16]{0:T(128)S(1)}, f32[16]{0:T(128)}, u32[]{:S(2)}) copy-start(f32[16]{0:T(128)} %param.17) | copy-start | bytes 196
  2.7 13.7 %collective-permute-start = (f32[4,1,32,512]{3,2,1,0:T(8,128)}, f32[4,1,32,512]{3,2,1,0:T(8,128)}, u32[]{:S(2)}, u32[]{:S(2)}) collective-permute-start(f32[4,1,32,512]{3,2,1,0:T(8,128)} %get-tuple-element.520), channel_id=1, source_target_pairs={{0,4},{4,8},{8,12},{12,16},{16,20},{20,24},{24,28},{1,5},{5,9},{9,... | collective-permute-start | bytes 786440 | tf_op jit(solution)/shard_map/ppermute | solution.py:16
  5.8 10.6 %collective-permute-start.1 = (f32[4,1,32,512]{3,2,1,0:T(8,128)}, f32[4,1,32,512]{3,2,1,0:T(8,128)}, u32[]{:S(2)}, u32[]{:S(2)}) collective-permute-start(f32[4,1,32,512]{3,2,1,0:T(8,128)} %get-tuple-element.521), channel_id=1, source_target_pairs={{4,0},{8,4},{12,8},{16,12},{20,16},{24,20},{28,24},{5,1},{9,5},{13... | collective-permute-start | bytes 786440 | tf_op jit(solution)/shard_map/ppermute | solution.py:19
  7.7 7.0 %collective-permute-start.4 = (f32[1]{0:T(128)}, f32[1]{0:T(128)}, u32[]{:S(2)}, u32[]{:S(2)}) collective-permute-start(f32[1]{0:T(128)} %get-tuple-element.546), channel_id=1, source_target_pairs={{4,0},{8,4},{12,8},{16,12},{20,16},{24,20},{28,24},{5,1},{9,5},{13... | collective-permute-start | bytes 20 | tf_op jit(solution)/shard_map/ppermute | solution.py:19
  9.0 6.0 %collective-permute-start.5 = (f32[1]{0:T(128)}, f32[1]{0:T(128)}, u32[]{:S(2)}, u32[]{:S(2)}) collective-permute-start(f32[1]{0:T(128)} %get-tuple-element.547), channel_id=1, source_target_pairs={{0,4},{4,8},{8,12},{12,16},{16,20},{20,24},{24,28},{1,5},{5,9},{9,... | collective-permute-start | bytes 20 | tf_op jit(solution)/shard_map/ppermute | solution.py:16
  14.7 15.3 %copy-start.4 = (f32[16,32,512]{2,1,0:T(8,128)S(1)}, f32[16,32,512]{2,1,0:T(8,128)}, u32[]{:S(2)}) copy-start(f32[16,32,512]{2,1,0:T(8,128)} %param.13) | copy-start | bytes 3145732
  17.9 6.9 %collective-permute-start.2 = (f32[4,18,1,512]{3,2,1,0:T(1,128)S(1)}, f32[4,18,1,512]{3,2,1,0:T(1,128)S(1)}, u32[]{:S(2)}, u32[]{:S(2)}) collective-permute-start(f32[4,18,1,512]{3,2,1,0:T(1,128)S(1)} %get-tuple-element.518), channel_id=1, source_target_pairs={{0,1},{1,2},{2,3},{4,5},{5,6},{6,7},{8,9},{9,10},{10,11},{12,13},{... | collective-permute-start | bytes 442376 | tf_op jit(solution)/shard_map/ppermute | solution.py:16
  21.3 8.7 %collective-permute-start.3 = (f32[4,18,1,512]{3,2,1,0:T(1,128)S(1)}, f32[4,18,1,512]{3,2,1,0:T(1,128)S(1)}, u32[]{:S(2)}, u32[]{:S(2)}) collective-permute-start(f32[4,18,1,512]{3,2,1,0:T(1,128)S(1)} %get-tuple-element.519), channel_id=1, source_target_pairs={{1,0},{2,1},{3,2},{5,4},{6,5},{7,6},{9,8},{10,9},{11,10},{13,12},{... | collective-permute-start | bytes 442376 | tf_op jit(solution)/shard_map/ppermute | solution.py:19
  53.4 1.6 copy-start
  56.1 2.8 %copy-start.5 = (f32[16,32,512]{2,1,0:T(8,128)}, f32[16,32,512]{2,1,0:T(8,128)S(1)}, u32[]{:S(2)}) copy-start(f32[16,32,512]{2,1,0:T(8,128)S(1)} %get-tuple-element.505) | copy-start | bytes 3145732
  56.1 2.8 %copy-start.6 = (f32[16,32,512]{2,1,0:T(8,128)}, f32[16,32,512]{2,1,0:T(8,128)S(1)}, u32[]{:S(2)}) copy-start(f32[16,32,512]{2,1,0:T(8,128)S(1)} %get-tuple-element.506) | copy-start | bytes 3145732
  56.2 2.8 %copy-start.7 = (f32[16,32,512]{2,1,0:T(8,128)}, f32[16,32,512]{2,1,0:T(8,128)S(1)}, u32[]{:S(2)}) copy-start(f32[16,32,512]{2,1,0:T(8,128)S(1)} %get-tuple-element.504) | copy-start | bytes 3145732
  57.4 2.6 %slice-start = ((f32[16,3,32,512]{3,2,1,0:T(8,128)}), f32[15,3,32,512]{3,2,1,0:T(8,128)S(1)}, s32[]{:S(2)}) async-start(f32[16,3,32,512]{3,2,1,0:T(8,128)} %copy-done), calls=%async_computation.2 | async-start | bytes 5898240 | tf_op jit(solution)/shard_map/slice | solution.py:144
  165.4 3.5 %collective-permute-start.6 = (f32[5,32,512]{2,1,0:T(8,128)S(1)}, f32[5,32,512]{2,1,0:T(8,128)S(1)}, u32[]{:S(2)}, u32[]{:S(2)}) collective-permute-start(f32[5,32,512]{2,1,0:T(8,128)S(1)} %slice_bitcast_fusion.2), channel_id=1, source_target_pairs={{4,0},{8,4},{12,8},{16,12},{20,16},{24,20},{28,24},{5,1},{9,5},{13... | collective-permute-start | bytes 983048 | tf_op jit(solution)/shard_map/ppermute | solution.py:27
  172.4 22.2 %all-to-all-start = ((f32[1,6,8,2048]{3,0,1,2:T(1,128)}), f32[1,6,8,2048]{3,0,1,2:T(1,128)S(1)}, u32[]{:S(2)}, u32[]{:S(2)}) async-start(f32[1,6,8,2048]{3,0,1,2:T(1,128)} %copy.45), calls=%async_computation | async-start | bytes 786432 | tf_op jit(solution)/shard_map/all_to_all | solution.py:164
  198.0 15.9 %all-to-all-start.1 = ((f32[8,6,1,2048]{3,2,1,0:T(1,128)}), f32[8,6,1,2048]{3,2,1,0:T(1,128)S(1)}, u32[]{:S(2)}, u32[]{:S(2)}) async-start(f32[8,6,1,2048]{3,2,1,0:T(1,128)} %fusion.73), calls=%async_computation.1 | async-start | bytes 786432 | tf_op jit(solution)/shard_map/all_to_all | solution.py:168
where the time goes:
time: 222 us; the launch traced here: 219 us
  other arithmetic  123 us (55%)
  waiting for transfers between devices  33.1 us (15%)
  local copies, waits for them, and re-layouts  31 us (14%)
  starting transfers between devices  30.4 us (14%)
    dynamic_update_slice x69, other arithmetic, thomas(): lax.scan(forward, start, (sub_coef, diag_coef, sup_coef, right_side))  83.4 us
    another operation x4, other arithmetic, explicit_terms(): return (jnp.stack(sides, axis=1), below_coef, above_coef)  14.5 us
    mul x15, local copies, waits for them, and re-layouts, backward(): result = value_row - ratio_row[None] * after  12.7 us
    all_to_all x1, waiting for transfers between devices, per_device(): lax.all_to_all(line_rows, 'gx', split_axis=2, concat_axis=0, tiled=True)  12.5 us
    ppermute x3, starting transfers between devices, padded_2(): lax.ppermute(lax.slice_in_dim(block, block.shape[dim] - width, None, axis...  12.2 us
    all_to_all x1, waiting for transfers between devices, per_device(): lax.all_to_all(paired, 'gx', split_axis=0, concat_axis=2, tiled=True)  10.8 us
    all_to_all x1, starting transfers between devices, per_device(): lax.all_to_all(line_rows, 'gx', split_axis=2, concat_axis=0, tiled=True)  9.62 us
    another operation x4, local copies, waits for them, and re-layouts  5.93 us
  transfers between devices with their start and end apart: 9, of which 6 were waited for; matrix products, arithmetic and copies ran while one was open for 2% of the time, Pallas kernels for 0%

commit v1 on v0

v1 whole, which is shorter than its diff:
```python
import functools

import jax
import jax.numpy as jnp
from jax import lax
from jax.experimental import pallas as pl
from jax.experimental.pallas import tpu as pltpu
from jax.sharding import PartitionSpec as P

time_step = 0.0125
face_factor = 2.0

LANES = 128
ROWS = 8
PAD = 8
FIELDS = 4
MESH = pl.DeviceIdType.MESH


def kernel(
    nx, ny,
    u_ref, v_ref, w_ref, nu_ref, width_ref,
    u_out, v_out, w_out,
    F, wv, span_inv, below_c, above_c, XH, ES, ER, CR, V, TP, PR, PS, SR, SS, O,
    local_sem, x_send, x_recv, y_send, y_recv, c_send, c_recv, w_send, w_recv,
    p_send, p_recv, s_send, s_recv, o_sem,
):
    X, Y, Z = u_ref.shape
    T = Z // LANES
    chunks = Y // ROWS
    gx = lax.axis_index("gx")
    gy = lax.axis_index("gy")
    has_x = (gx > 0, gx < nx - 1)
    has_y = (gy > 0, gy < ny - 1)
    inputs = (u_ref, v_ref, w_ref, nu_ref)
    outputs = (u_out, v_out, w_out)

    def local_copies():
        return [
            pltpu.make_async_copy(
                inputs[f].at[:, :, t * LANES:(t + 1) * LANES],
                F.at[f, 1:X + 1, t, PAD:PAD + Y, :],
                local_sem.at[f, t],
            )
            for f in range(FIELDS) for t in range(T)
        ]

    for copy in local_copies():
        copy.start()

    barrier = pltpu.get_barrier_semaphore()
    partners = []
    for dx in (-1, 0, 1):
        for dy in (-1, 0, 1):
            if dx == 0 and dy == 0:
                continue
            ok = None
            if dx:
                ok = has_x[(dx + 1) // 2]
            if dy:
                oky = has_y[(dy + 1) // 2]
                ok = oky if ok is None else jnp.logical_and(ok, oky)
            partners.append((dx, dy, ok))
    for dx, dy, ok in partners:
        @pl.when(ok)
        def _():
            pl.semaphore_signal(barrier, inc=1, device_id=(gx + dx, gy + dy), device_id_type=MESH)
    near_x = has_x[0].astype(jnp.int32) + has_x[1].astype(jnp.int32)
    near_y = has_y[0].astype(jnp.int32) + has_y[1].astype(jnp.int32)
    pl.semaphore_wait(barrier, near_x + near_y + near_x * near_y)

    def x_copy(s, f):
        return pltpu.make_async_remote_copy(
            src_ref=inputs[f].at[(X - 1) * s],
            dst_ref=XH.at[1 - s, f],
            send_sem=x_send.at[s, f], recv_sem=x_recv.at[1 - s, f],
            device_id=(gx + 2 * s - 1, gy), device_id_type=MESH,
        )

    def w_copy(s):
        return pltpu.make_async_remote_copy(
            src_ref=wv.at[X if s else 1],
            dst_ref=wv.at[0 if s else X + 1],
            send_sem=w_send.at[s], recv_sem=w_recv.at[1 - s],
            device_id=(gx + 2 * s - 1, gy), device_id_type=MESH,
        )

    def y_copy(s):
        return pltpu.make_async_remote_copy(
            src_ref=ES.at[s], dst_ref=ER.at[1 - s],
            send_sem=y_send.at[s], recv_sem=y_recv.at[1 - s],
            device_id=(gx, gy + 2 * s - 1), device_id_type=MESH,
        )

    def c_copy(a, b):
        return pltpu.make_async_remote_copy(
            src_ref=ES.at[b, 0:2, (X - 1) * a], dst_ref=CR.at[1 - a, 1 - b],
            send_sem=c_send.at[a, b], recv_sem=c_recv.at[1 - a, 1 - b],
            device_id=(gx + 2 * a - 1, gy + 2 * b - 1), device_id_type=MESH,
        )

    for s in (0, 1):
        @pl.when(has_x[s])
        def _():
            for f in range(FIELDS):
                x_copy(s, f).start()

    for i in range(X):
        wv[i + 1] = jnp.full((ROWS, LANES), width_ref[i], jnp.float32)
    for s in (0, 1):
        @pl.when(has_x[s])
        def _():
            w_copy(s).start()

        @pl.when(jnp.logical_not(has_x[s]))
        def _():
            wv[(X + 1) * s] = jnp.zeros((ROWS, LANES), jnp.float32)

    for copy in local_copies():
        copy.wait()

    edge = (PAD, PAD + Y - 1)
    outer = (PAD - 1, PAD + Y)

    def pack(f, carry):
        for s in (0, 1):
            ES[s, f] = F[f, 1:X + 1, :, edge[s]:edge[s] + 1, :]
        return carry

    lax.fori_loop(0, FIELDS, pack, 0)
    for s in (0, 1):
        @pl.when(has_y[s])
        def _():
            y_copy(s).start()
    for a in (0, 1):
        for b in (0, 1):
            @pl.when(jnp.logical_and(has_x[a], has_y[b]))
            def _():
                c_copy(a, b).start()

    for s in (0, 1):
        @pl.when(jnp.logical_not(has_y[s]))
        def _():
            def fill(f, carry):
                F[f, :, :, outer[s]:outer[s] + 1, :] = jnp.zeros((X + 2, T, 1, LANES), jnp.float32)
                return carry
            lax.fori_loop(0, FIELDS, fill, 0)

        @pl.when(jnp.logical_not(has_x[s]))
        def _():
            def fill(f, carry):
                F[f, (X + 1) * s] = jnp.zeros((T, Y + 2 * PAD, LANES), jnp.float32)
                return carry
            lax.fori_loop(0, FIELDS, fill, 0)

    for s in (0, 1):
        @pl.when(has_x[s])
        def _():
            w_copy(s).wait_send()
            w_copy(1 - s).wait_recv()
            for f in range(FIELDS):
                x_copy(s, f).wait_send()
                x_copy(1 - s, f).wait_recv()

            def spread(f, carry):
                for t in range(T):
                    F[f, (X + 1) * s, t, PAD:PAD + Y, :] = XH[s, f, :, t * LANES:(t + 1) * LANES]
                return carry
            lax.fori_loop(0, FIELDS, spread, 0)

    for i in range(X):
        low, mid, high = wv[i], wv[i + 1], wv[i + 2]
        span_inv[i] = 1.0 / (0.5 * low + mid + 0.5 * high)
        below_c[i] = time_step / (mid * (low + mid))
        above_c[i] = time_step / (mid * (mid + high))

    lane = lax.broadcasted_iota(jnp.int32, (T, ROWS, LANES), 2)
    first_lane = lane == 0
    last_lane = lane == LANES - 1
    zero_tile = jnp.zeros((1, ROWS, LANES), jnp.float32)

    def z_next(a):
        r = pltpu.roll(a, LANES - 1, 2)
        after = jnp.concatenate([r[1:], zero_tile], axis=0)
        return jnp.where(last_lane, after, r)

    def z_prev(a):
        r = pltpu.roll(a, 1, 2)
        before = jnp.concatenate([zero_tile, r[:-1]], axis=0)
        return jnp.where(first_lane, before, r)

    def z_diff(a):
        return z_next(a) - z_prev(a)

    def compute_chunk(yc):
        base = PAD + yc * ROWS

        def ld(f, i, dy=0):
            return F[f, i, :, pl.ds(base + dy, ROWS), :]

        def flux_uy(i):
            return ld(3, i) * (ld(0, i, 1) - ld(0, i, -1))

        def row(i, state):
            (fuy_prev, fuy_now, fuz_prev, fuz_now, u_zn, u_zp,
             c, v0, v1, v2, l, f0, f1, f2, fl, fr) = state
            inv_s = span_inv[i][None]
            nu0, nu_xp, nu_xm = ld(3, i + 1), ld(3, i + 2), ld(3, i)
            nu_yp, nu_ym = ld(3, i + 1, 1), ld(3, i + 1, -1)
            u_next_row = ld(0, i + 2)
            u_zn_next, u_zp_next = z_next(u_next_row), z_prev(u_next_row)
            fuy_next = flux_uy(i + 2)
            fuz_next = nu_xp * (u_zn_next - u_zp_next)

            face_yp, face_ym = nu0 + nu_yp, nu0 + nu_ym
            face_zp, face_zm = nu0 + z_next(nu0), nu0 + z_prev(nu0)
            face_sum = (face_yp + face_ym) + (face_zp + face_zm)
            mid = [ld(f, i + 1) for f in range(3)]
            u_scaled = mid[0] * inv_s

            x_dw = ld(2, i + 2) - ld(2, i)
            v_yp, v_ym = ld(1, i + 1, 1), ld(1, i + 1, -1)
            w_yp, w_ym = ld(2, i + 1, 1), ld(2, i + 1, -1)
            cross_u = inv_s * (
                nu_yp * (ld(1, i + 2, 1) - ld(1, i, 1))
                - nu_ym * (ld(1, i + 2, -1) - ld(1, i, -1))
                + z_diff(nu0 * x_dw)
            )
            cross_v = inv_s * (fuy_next - fuy_prev) + z_diff(nu0 * (w_yp - w_ym))
            cross_w = inv_s * (fuz_next - fuz_prev) + (nu_yp * z_diff(v_yp) - nu_ym * z_diff(v_ym))

            def side(f, cross, yp, ym, zn, zp, x_d):
                q = mid[f]
                advect = u_scaled * x_d + mid[1] * (yp - ym) + mid[2] * (zn - zp)
                spread = (face_yp * yp + face_ym * ym) + (face_zp * zn + face_zm * zp) - face_sum * q
                return q + time_step * (face_factor * spread + (cross - advect))

            r0 = side(0, cross_u, ld(0, i + 1, 1), ld(0, i + 1, -1), u_zn, u_zp, u_next_row - ld(0, i))
            r1 = side(1, cross_v, v_yp, v_ym, z_next(mid[1]), z_prev(mid[1]), ld(1, i + 2) - ld(1, i))
            r2 = side(2, cross_w, w_yp, w_ym, z_next(mid[2]), z_prev(mid[2]), x_dw)

            below = below_c[i][None] * (nu0 + nu_xm)
            above = above_c[i][None] * (nu0 + nu_xp)
            inv = 1.0 / (1.0 + above + below * (1.0 - c))
            c = above * inv
            lower = below * inv
            v0 = r0 * inv + lower * v0
            v1 = r1 * inv + lower * v1
            v2 = r2 * inv + lower * v2
            l = lower * l
            for k, value in enumerate((v0, v1, v2, l, c)):
                V[k, yc, i] = value
            f0 = f0 + fr * v0
            f1 = f1 + fr * v1
            f2 = f2 + fr * v2
            fl = fl + fr * l
            fr = fr * c
            return (fuy_now, fuy_next, fuz_now, fuz_next, u_zn_next, u_zp_next,
                    c, v0, v1, v2, l, f0, f1, f2, fl, fr)

        u_low, u_mid = ld(0, 0), ld(0, 1)
        u_zn, u_zp = z_next(u_mid), z_prev(u_mid)
        zero = jnp.zeros((T, ROWS, LANES), jnp.float32)
        one = jnp.ones((T, ROWS, LANES), jnp.float32)
        state = (flux_uy(0), flux_uy(1), ld(3, 0) * z_diff(u_low), ld(3, 1) * (u_zn - u_zp), u_zn, u_zp,
                 zero, zero, zero, zero, one, zero, zero, zero, zero, one)
        state = lax.fori_loop(0, X, row, state)
        c, v0, v1, v2, l, f0, f1, f2, fl, fr = state[6:]
        for k, value in enumerate((f0, f1, f2, fl, fr, v0, v1, v2, l, c)):
            TP[yc, k] = value

    def inner(k, carry):
        compute_chunk(k)
        return carry

    if chunks > 2:
        lax.fori_loop(1, chunks - 1, inner, 0)

    for s in (0, 1):
        @pl.when(has_y[s])
        def _():
            y_copy(s).wait_send()
            y_copy(1 - s).wait_recv()

            def spread(f, carry):
                F[f, 1:X + 1, :, outer[s]:outer[s] + 1, :] = ER[s, f]
                return carry
            lax.fori_loop(0, FIELDS, spread, 0)
    for a in (0, 1):
        for b in (0, 1):
            @pl.when(jnp.logical_and(has_x[a], has_y[b]))
            def _():
                c_copy(a, b).wait_send()
                c_copy(1 - a, 1 - b).wait_recv()
                for f in (0, 1):
                    F[f, (X + 1) * a, :, outer[b]:outer[b] + 1, :] = CR[a, b, f]

    ends = min(2, chunks)

    def outermost(k, carry):
        compute_chunk(k * (chunks - 1))
        return carry

    lax.fori_loop(0, ends, outermost, 0)

    def p_copy(yc):
        return pltpu.make_async_remote_copy(
            src_ref=PS.at[yc], dst_ref=PR.at[yc],
            send_sem=p_send.at[yc], recv_sem=p_recv.at[yc],
            device_id=(gx + 1, gy), device_id_type=MESH,
        )

    def s_copy(yc):
        return pltpu.make_async_remote_copy(
            src_ref=SS.at[yc], dst_ref=SR.at[yc],
            send_sem=s_send.at[yc], recv_sem=s_recv.at[yc],
            device_id=(gx - 1, gy), device_id_type=MESH,
        )

    @pl.when(gx == 0)
    def _():
        PR[...] = jnp.zeros(PR.shape, jnp.float32)

    @pl.when(gx == nx - 1)
    def _():
        SR[...] = jnp.zeros(SR.shape, jnp.float32)

    def relate(yc, came, give, near, far):
        near0, near_own, near_other = near
        far0, far_own, far_other = far
        q = came[yc, 3]
        own = TP[yc, near_own]
        m = q / (1.0 - own * q)
        gain = TP[yc, far_own]
        for k in range(3):
            p = came[yc, k]
            give[yc, k] = TP[yc, far0 + k] + gain * (p + m * (TP[yc, near0 + k] + own * p))
        give[yc, 3] = TP[yc, far_other] + gain * m * TP[yc, near_other]

    def back(yc):
        t_p, q_p = SR[yc, 3], PS[yc, 3]
        t_s, q_s = PR[yc, 3], SS[yc, 3]
        high_inv = 1.0 / (1.0 - t_p * q_p)
        low_inv = 1.0 / (1.0 - t_s * q_s)
        high = [(SR[yc, k] + t_p * PS[yc, k]) * high_inv for k in range(3)]
        low = [(PR[yc, k] + t_s * SS[yc, k]) * low_inv for k in range(3)]

        def row(n, now):
            i = X - 1 - n
            l, c = V[3, yc, i], V[4, yc, i]
            now = tuple(V[k, yc, i] + l * low[k] + c * now[k] for k in range(3))
            for k in range(3):
                for t in range(T):
                    O[k, i, pl.ds(pl.multiple_of(yc * ROWS, ROWS), ROWS), t * LANES:(t + 1) * LANES] = now[k][t]
            return now

        lax.fori_loop(0, X, row, tuple(high))
        for k in range(3):
            out_copy(k, yc).start()

    def out_copy(k, yc):
        part = pl.ds(pl.multiple_of(yc * ROWS, ROWS), ROWS)
        return pltpu.make_async_copy(O.at[k, :, part, :], outputs[k].at[:, part, :], o_sem.at[k, yc])

    def link_step(step, carry):
        up = step - gx
        down = step - (nx - 1 - gx)

        @pl.when(jnp.logical_and(up >= 0, up < chunks))
        def _():
            @pl.when(has_x[0])
            def _():
                p_copy(up).wait_recv()
            relate(up, PR, PS, (0, 3, 4), (5, 8, 9))

            @pl.when(has_x[1])
            def _():
                p_copy(up).start()

        @pl.when(jnp.logical_and(down >= 0, down < chunks))
        def _():
            @pl.when(has_x[1])
            def _():
                s_copy(down).wait_recv()
            relate(down, SR, SS, (5, 9, 8), (0, 4, 3))

            @pl.when(has_x[0])
            def _():
                s_copy(down).start()

        ready = step - (nx - 1)

        @pl.when(ready >= 0)
        def _():
            back(ready)

        return carry

    lax.fori_loop(0, nx - 1 + chunks, link_step, 0)

    for yc in range(chunks):
        @pl.when(has_x[1])
        def _():
            p_copy(yc).wait_send()

        @pl.when(has_x[0])
        def _():
            s_copy(yc).wait_send()
        for k in range(3):
            out_copy(k, yc).wait()


def per_device(nx, ny, u_velocity, v_velocity, w_velocity, viscosity, cell_width):
    X, Y, Z = u_velocity.shape
    T = Z // LANES
    chunks = Y // ROWS
    f32 = jnp.float32
    dma = pltpu.SemaphoreType.DMA
    anywhere = pl.BlockSpec(memory_space=pl.ANY)
    out = jax.ShapeDtypeStruct((X, Y, Z), f32)
    return pl.pallas_call(
        functools.partial(kernel, nx, ny),
        out_shape=(out, out, out),
        in_specs=[anywhere] * 4 + [pl.BlockSpec(memory_space=pltpu.SMEM)],
        out_specs=(anywhere,) * 3,
        scratch_shapes=[
            pltpu.VMEM((FIELDS, X + 2, T, Y + 2 * PAD, LANES), f32),
            pltpu.VMEM((X + 2, ROWS, LANES), f32),
            pltpu.VMEM((X, ROWS, LANES), f32),
            pltpu.VMEM((X, ROWS, LANES), f32),
            pltpu.VMEM((X, ROWS, LANES), f32),
            pltpu.VMEM((2, FIELDS, Y, Z), f32),
            pltpu.VMEM((2, FIELDS, X, T, 1, LANES), f32),
            pltpu.VMEM((2, FIELDS, X, T, 1, LANES), f32),
            pltpu.VMEM((2, 2, 2, T, 1, LANES), f32),
            pltpu.VMEM((5, chunks, X, T, ROWS, LANES), f32),
            pltpu.VMEM((chunks, 10, T, ROWS, LANES), f32),
            pltpu.VMEM((chunks, 4, T, ROWS, LANES), f32),
            pltpu.VMEM((chunks, 4, T, ROWS, LANES), f32),
            pltpu.VMEM((chunks, 4, T, ROWS, LANES), f32),
            pltpu.VMEM((chunks, 4, T, ROWS, LANES), f32),
            pltpu.VMEM((3, X, Y, Z), f32),
            dma((FIELDS, T)),
            dma((2, FIELDS)), dma((2, FIELDS)),
            dma((2,)), dma((2,)),
            dma((2, 2)), dma((2, 2)),
            dma((2,)), dma((2,)),
            dma((chunks,)), dma((chunks,)),
            dma((chunks,)), dma((chunks,)),
            dma((3, chunks)),
        ],
        compiler_params=pltpu.CompilerParams(
            collective_id=0, has_side_effects=True, vmem_limit_bytes=48 * 1024 * 1024
        ),
    )(u_velocity, v_velocity, w_velocity, viscosity, cell_width)


def solution(mesh):
    spec = P("gx", "gy", None)
    return jax.shard_map(
        functools.partial(per_device, mesh.shape["gx"], mesh.shape["gy"]),
        mesh=mesh,
        in_specs=(spec, spec, spec, spec, P("gx")),
        out_specs=(spec, spec, spec),
        check_vma=False,
    )
```

time: 222 us -> 47.9 us (0.22); the launches traced: 219 us -> 47.7 us
  other arithmetic: 123 us -> 0 us
  Pallas kernels: 0 us -> 41 us
  waiting for transfers between devices: 33.1 us -> 0 us
  starting transfers between devices: 30.4 us -> 0 us
  local copies, waits for them, and re-layouts: 31 us -> 6.01 us
    dynamic_update_slice x69 -> x0, other arithmetic: 83.4 us -> none  [thomas(): lax.scan(forward, start, (sub_coef, diag_coef, sup_coef, right_side))]
    pallas_call x0 -> x1, Pallas kernels: none -> 41 us  [per_device(): pl.pallas_call(functools.partial(kernel, nx, ny), out_shape=(out, out, ou...]
    all_to_all x2 -> x0, waiting for transfers between devices: 23.3 us -> none  [the longest x1 12.5 us: per_device(): lax.all_to_all(line_rows, 'gx', split_axis=2, concat_axis=0, tiled=True)]
    ppermute x7 -> x0, starting transfers between devices: 17.3 us -> none  [the longest x3 12.2 us: padded_2(): lax.ppermute(lax.slice_in_dim(block, block.shape[dim] - width, None, axis...]
    mul x18 -> x0, local copies, waits for them, and re-layouts: 14.5 us -> none  [the longest x15 12.7 us: backward(): result = value_row - ratio_row[None] * after]
    another operation x4 -> x0, other arithmetic: 14.5 us -> none  [explicit_terms(): return (jnp.stack(sides, axis=1), below_coef, above_coef)]
    all_to_all x2 -> x0, starting transfers between devices: 13.1 us -> none  [the longest x1 9.62 us: per_device(): lax.all_to_all(line_rows, 'gx', split_axis=2, concat_axis=0, tiled=True)]
    ppermute x7 -> x0, waiting for transfers between devices: 9.79 us -> none  [the longest x3 5.22 us: padded_2(): lax.ppermute(lax.slice_in_dim(block, 0, width, axis=dim), axis, backward)]
  transfers between devices with their start and end apart: 9 -> 0, of which waited for: 6 -> 0; matrix products, arithmetic and copies ran while one was open for 2% -> 0% of each run, Pallas kernels for 0% -> 0%
where the time goes in v1:
time: 47.9 us; the launch traced here: 47.7 us
  Pallas kernels  41 us (86%)
  local copies, waits for them, and re-layouts  6.01 us (13%)
  between operations  0.65 us (1%)
    pallas_call x1, Pallas kernels, per_device(): pl.pallas_call(functools.partial(kernel, nx, ny), out_shape=(out, out, ou...  41 us
    unnamed x9, local copies, waits for them, and re-layouts  6.01 us

profile of v1, /device:TPU:0, one launch (start us, length us, event | category | flops | bytes accessed | tf_op | source)
XLA Modules:
  0.0 47.7 jit_solution(82584771277165312)
XLA Ops:
  0.6 0.0 copy-start
  0.6 1.2 %copy-done = f32[16,32,512]{2,1,0:T(8,128)S(1)} copy-done((f32[16,32,512]{2,1,0:T(8,128)S(1)}, f32[16,32,512]{2,1,0:T(8,128)}, u32[]{:S(2)}) %copy-start) | copy-done | bytes 1048600
  1.9 0.0 copy-start.1
  1.9 1.2 %copy-done.1 = f32[16,32,512]{2,1,0:T(8,128)S(1)} copy-done((f32[16,32,512]{2,1,0:T(8,128)S(1)}, f32[16,32,512]{2,1,0:T(8,128)}, u32[]{:S(2)}) %copy-start.1) | copy-done | bytes 1048600
  3.1 0.0 copy-start.2
  3.1 0.7 %copy-done.2 = f32[16]{0:T(128)S(1)} copy-done((f32[16]{0:T(128)S(1)}, f32[16]{0:T(128)}, u32[]{:S(2)}) %copy-start.2) | copy-done | bytes 88
  3.7 41.0 %shard_map.76 = (f32[16,32,512]{2,1,0:T(8,128)S(1)}, f32[16,32,512]{2,1,0:T(8,128)S(1)}, f32[16,32,512]{2,1,0:T(8,128)S(1)}) custom-call(f32[16,32,512]{2,1,0:T(8,128)S(1)} %copy-done, f32[16,32,512]{2,1,0:T(8,128)S(1)} %copy-done.1, f32[16,32,512]{2,1,0:T(8,128)} %w_ref.1, f32[16,32,512]{2,1,0:T(8,128)} %nu_ref.1, f32[16]{0:T(128)S(1)} %copy-done.2), custom_call_target="tpu_custom_call" | custom-call | tf_op jit(solution)/shard_map/pallas_call | solution.py:421
  44.8 1.0 %copy.11 = f32[16,32,512]{2,1,0:T(8,128)} copy(f32[16,32,512]{2,1,0:T(8,128)S(1)} %get-tuple-element.6) | data formatting | bytes 2097152
  45.7 1.0 %copy.12 = f32[16,32,512]{2,1,0:T(8,128)} copy(f32[16,32,512]{2,1,0:T(8,128)S(1)} %get-tuple-element.7) | data formatting | bytes 2097152
  46.7 1.0 %copy.13 = f32[16,32,512]{2,1,0:T(8,128)} copy(f32[16,32,512]{2,1,0:T(8,128)S(1)} %get-tuple-element.8) | data formatting | bytes 2097152
Async XLA Ops:
  0.6 1.2 %copy-start = (f32[16,32,512]{2,1,0:T(8,128)S(1)}, f32[16,32,512]{2,1,0:T(8,128)}, u32[]{:S(2)}) copy-start(f32[16,32,512]{2,1,0:T(8,128)} %u_ref.1) | copy-start | bytes 3145732
  1.9 1.2 %copy-start.1 = (f32[16,32,512]{2,1,0:T(8,128)S(1)}, f32[16,32,512]{2,1,0:T(8,128)}, u32[]{:S(2)}) copy-start(f32[16,32,512]{2,1,0:T(8,128)} %v_ref.1) | copy-start | bytes 3145732
  3.1 0.7 %copy-start.2 = (f32[16]{0:T(128)S(1)}, f32[16]{0:T(128)}, u32[]{:S(2)}) copy-start(f32[16]{0:T(128)} %width_ref.1) | copy-start | bytes 196

commit v2 on v1

--- a/solution.py
+++ b/solution.py
@@ -19,11 +19,11 @@
 
 def kernel(
     nx, ny,
-    u_ref, v_ref, w_ref, nu_ref, width_ref,
-    u_out, v_out, w_out,
-    F, wv, span_inv, below_c, above_c, XH, ES, ER, CR, V, TP, PR, PS, SR, SS, O,
-    local_sem, x_send, x_recv, y_send, y_recv, c_send, c_recv, w_send, w_recv,
-    p_send, p_recv, s_send, s_recv, o_sem,
+    u_ref, v_ref, w_ref, nu_ref, width_in,
+    V, ends_out,
+    F, wv, span_inv, below_c, above_c, XH, ES, ER, CR, TP, PR, PS, SR, SS, width_ref,
+    width_sem, local_sem, x_send, x_recv, y_send, y_recv, c_send, c_recv, w_send, w_recv,
+    p_send, p_recv, s_send, s_recv,
 ):
     X, Y, Z = u_ref.shape
     T = Z // LANES
@@ -33,7 +33,6 @@
     has_x = (gx > 0, gx < nx - 1)
     has_y = (gy > 0, gy < ny - 1)
     inputs = (u_ref, v_ref, w_ref, nu_ref)
-    outputs = (u_out, v_out, w_out)
 
     def local_copies():
         return [
@@ -45,6 +44,8 @@
             for f in range(FIELDS) for t in range(T)
         ]
 
+    width_copy = pltpu.make_async_copy(width_in, width_ref, width_sem)
+    width_copy.start()
     for copy in local_copies():
         copy.start()
 
@@ -105,6 +106,7 @@
             for f in range(FIELDS):
                 x_copy(s, f).start()
 
+    width_copy.wait()
     for i in range(X):
         wv[i + 1] = jnp.full((ROWS, LANES), width_ref[i], jnp.float32)
     for s in (0, 1):
@@ -337,13 +339,75 @@
             give[yc, k] = TP[yc, far0 + k] + gain * (p + m * (TP[yc, near0 + k] + own * p))
         give[yc, 3] = TP[yc, far_other] + gain * m * TP[yc, near_other]
 
-    def back(yc):
+    def close(yc):
         t_p, q_p = SR[yc, 3], PS[yc, 3]
         t_s, q_s = PR[yc, 3], SS[yc, 3]
         high_inv = 1.0 / (1.0 - t_p * q_p)
         low_inv = 1.0 / (1.0 - t_s * q_s)
-        high = [(SR[yc, k] + t_p * PS[yc, k]) * high_inv for k in range(3)]
-        low = [(PR[yc, k] + t_s * SS[yc, k]) * low_inv for k in range(3)]
+        for k in range(3):
+            ends_out[yc, k] = (PR[yc, k] + t_s * SS[yc, k]) * low_inv
+            ends_out[yc, 3 + k] = (SR[yc, k] + t_p * PS[yc, k]) * high_inv
+
+    def pass_up(k, carry):
+        @pl.when(has_x[0])
+        def _():
+            p_copy(k).wait_recv()
+        relate(k, PR, PS, (0, 3, 4), (5, 8, 9))
+
+        @pl.when(has_x[1])
+        def _():
+            p_copy(k).start()
+        return carry
+
+    def pass_down(k, carry):
+        @pl.when(has_x[1])
+        def _():
+            s_copy(k).wait_recv()
+        relate(k, SR, SS, (5, 9, 8), (0, 4, 3))
+
+        @pl.when(has_x[0])
+        def _():
+            s_copy(k).start()
+        return carry
+
+    low_half = gx < nx // 2
+
+    @pl.when(low_half)
+    def _():
+        lax.fori_loop(0, chunks, pass_up, 0)
+        lax.fori_loop(0, chunks, pass_down, 0)
+
+    @pl.when(jnp.logical_not(low_half))
+    def _():
+        lax.fori_loop(0, chunks, pass_down, 0)
+        lax.fori_loop(0, chunks, pass_up, 0)
+
+    def close_step(yc, carry):
+        close(yc)
+        return carry
+
+    lax.fori_loop(0, chunks, close_step, 0)
+
+    for yc in range(chunks):
+        @pl.when(has_x[1])
+        def _():
+            p_copy(yc).wait_send()
+
+        @pl.when(has_x[0])
+        def _():
+            s_copy(yc).wait_send()
+
+
+def substitute(V, ends, u_out, v_out, w_out, O, o_sem):
+    _, chunks, X, T, _, _ = V.shape
+    outputs = (u_out, v_out, w_out)
+
+    def copy(k, yc):
+        part = pl.ds(pl.multiple_of(yc * ROWS, ROWS), ROWS)
+        return pltpu.make_async_copy(O.at[k, :, part, :], outputs[k].at[:, part, :], o_sem.at[k, yc])
+
+    def chunk(yc, carry):
+        low = [ends[yc, k] for k in range(3)]
 
         def row(n, now):
             i = X - 1 - n
@@ -354,60 +418,15 @@
                     O[k, i, pl.ds(pl.multiple_of(yc * ROWS, ROWS), ROWS), t * LANES:(t + 1) * LANES] = now[k][t]
             return now
 
-        lax.fori_loop(0, X, row, tuple(high))
+        lax.fori_loop(0, X, row, tuple(ends[yc, 3 + k] for k in range(3)))
         for k in range(3):
-            out_copy(k, yc).start()
-
-    def out_copy(k, yc):
-        part = pl.ds(pl.multiple_of(yc * ROWS, ROWS), ROWS)
-        return pltpu.make_async_copy(O.at[k, :, part, :], outputs[k].at[:, part, :], o_sem.at[k, yc])
-
-    def link_step(step, carry):
-        up = step - gx
-        down = step - (nx - 1 - gx)
-
-        @pl.when(jnp.logical_and(up >= 0, up < chunks))
-        def _():
-            @pl.when(has_x[0])
-            def _():
-                p_copy(up).wait_recv()
-            relate(up, PR, PS, (0, 3, 4), (5, 8, 9))
-
-            @pl.when(has_x[1])
-            def _():
-                p_copy(up).start()
-
-        @pl.when(jnp.logical_and(down >= 0, down < chunks))
-        def _():
-            @pl.when(has_x[1])
-            def _():
-                s_copy(down).wait_recv()
-            relate(down, SR, SS, (5, 9, 8), (0, 4, 3))
-
-            @pl.when(has_x[0])
-            def _():
-                s_copy(down).start()
-
-        ready = step - (nx - 1)
-
-        @pl.when(ready >= 0)
-        def _():
-            back(ready)
-
-        return carry
-
-    lax.fori_loop(0, nx - 1 + chunks, link_step, 0)
-
+            copy(k, yc).start()
+        return carry
+
+    lax.fori_loop(0, chunks, chunk, 0)
     for yc in range(chunks):
-        @pl.when(has_x[1])
-        def _():
-            p_copy(yc).wait_send()
-
-        @pl.when(has_x[0])
-        def _():
-            s_copy(yc).wait_send()
         for k in range(3):
-            out_copy(k, yc).wait()
+            copy(k, yc).wait()
 
 
 def per_device(nx, ny, u_velocity, v_velocity, w_velocity, viscosity, cell_width):
@@ -416,13 +435,17 @@
     chunks = Y // ROWS
     f32 = jnp.float32
     dma = pltpu.SemaphoreType.DMA
-    anywhere = pl.BlockSpec(memory_space=pl.ANY)
+    in_hbm = pl.BlockSpec(memory_space=pltpu.HBM)
+    in_vmem = pl.BlockSpec(memory_space=pltpu.VMEM)
     out = jax.ShapeDtypeStruct((X, Y, Z), f32)
-    return pl.pallas_call(
+    rows, ends = pl.pallas_call(
         functools.partial(kernel, nx, ny),
-        out_shape=(out, out, out),
-        in_specs=[anywhere] * 4 + [pl.BlockSpec(memory_space=pltpu.SMEM)],
-        out_specs=(anywhere,) * 3,
+        out_shape=(
+            jax.ShapeDtypeStruct((5, chunks, X, T, ROWS, LANES), f32),
+            jax.ShapeDtypeStruct((chunks, 6, T, ROWS, LANES), f32),
+        ),
+        in_specs=[in_hbm] * 5,
+        out_specs=(in_vmem,) * 2,
         scratch_shapes=[
             pltpu.VMEM((FIELDS, X + 2, T, Y + 2 * PAD, LANES), f32),
             pltpu.VMEM((X + 2, ROWS, LANES), f32),
@@ -433,26 +456,32 @@
             pltpu.VMEM((2, FIELDS, X, T, 1, LANES), f32),
             pltpu.VMEM((2, FIELDS, X, T, 1, LANES), f32),
             pltpu.VMEM((2, 2, 2, T, 1, LANES), f32),
-            pltpu.VMEM((5, chunks, X, T, ROWS, LANES), f32),
             pltpu.VMEM((chunks, 10, T, ROWS, LANES), f32),
             pltpu.VMEM((chunks, 4, T, ROWS, LANES), f32),
             pltpu.VMEM((chunks, 4, T, ROWS, LANES), f32),
             pltpu.VMEM((chunks, 4, T, ROWS, LANES), f32),
             pltpu.VMEM((chunks, 4, T, ROWS, LANES), f32),
-            pltpu.VMEM((3, X, Y, Z), f32),
-            dma((FIELDS, T)),
+            pltpu.SMEM((X,), f32),
+            dma, dma((FIELDS, T)),
             dma((2, FIELDS)), dma((2, FIELDS)),
             dma((2,)), dma((2,)),
             dma((2, 2)), dma((2, 2)),
             dma((2,)), dma((2,)),
             dma((chunks,)), dma((chunks,)),
             dma((chunks,)), dma((chunks,)),
-            dma((3, chunks)),
         ],
         compiler_params=pltpu.CompilerParams(
-            collective_id=0, has_side_effects=True, vmem_limit_bytes=48 * 1024 * 1024
+            collective_id=0, has_side_effects=True, vmem_limit_bytes=57 * 1024 * 1024
         ),
     )(u_velocity, v_velocity, w_velocity, viscosity, cell_width)
+    return pl.pallas_call(
+        substitute,
+        out_shape=(out, out, out),
+        in_specs=[in_vmem] * 2,
+        out_specs=(in_hbm,) * 3,
+        scratch_shapes=[pltpu.VMEM((3, X, Y, Z), f32), dma((3, chunks))],
+        compiler_params=pltpu.CompilerParams(vmem_limit_bytes=16 * 1024 * 1024),
+    )(rows, ends)
 
 
 def solution(mesh):

time: 47.9 us -> 45.5 us (0.950)
  local copies, waits for them, and re-layouts: 6.01 us -> 3.47 us
    unnamed x9 -> x4, local copies, waits for them, and re-layouts: 6.01 us -> 3.47 us
    pallas_call x1 -> x2, Pallas kernels: 41 us -> 41.2 us  [the longest x1 39.2 us: per_device(): pl.pallas_call(functools.partial(kernel, nx, ny), out_shape=(jax.ShapeDty...]
where the time goes in v2:
time: 45.5 us; the launch traced here: 45.3 us
  Pallas kernels  41.2 us (91%)
  local copies, waits for them, and re-layouts  3.47 us (8%)
  between operations  0.65 us (1%)
    pallas_call x1, Pallas kernels, per_device(): pl.pallas_call(functools.partial(kernel, nx, ny), out_shape=(jax.ShapeDty...  39.2 us
    unnamed x4, local copies, waits for them, and re-layouts  3.47 us
    pallas_call x1, Pallas kernels, per_device(): pl.pallas_call(substitute, out_shape=(out, out, out), in_specs=[in_vmem]...  1.95 us

profile of v2, /device:TPU:0, one launch (start us, length us, event | category | flops | bytes accessed | tf_op | source)
XLA Modules:
  0.0 45.3 jit_solution(8665719665367004378)
XLA Ops:
  0.6 39.2 %shard_map.76 = (f32[5,4,16,4,8,128]{5,4,3,2,1,0:T(8,128)}, f32[4,6,4,8,128]{4,3,2,1,0:T(8,128)}) custom-call(f32[16,32,512]{2,1,0:T(8,128)} %u_ref.1, f32[16,32,512]{2,1,0:T(8,128)} %v_ref.1, f32[16,32,512]{2,1,0:T(8,128)} %w_ref.1, f32[16,32,512]{2,1,0:T(8,128)} %nu_ref.1, f32[16]{0:T(128)} %width_in.1), custom_call_target="tpu_custom_call" | custom-call | tf_op jit(solution)/shard_map/pallas_call | solution.py:441
  39.9 0.0 copy-start
  39.9 2.5 %copy-done = f32[5,4,16,4,8,128]{5,4,3,2,1,0:T(8,128)S(1)} copy-done((f32[5,4,16,4,8,128]{5,4,3,2,1,0:T(8,128)S(1)}, f32[5,4,16,4,8,128]{5,4,3,2,1,0:T(8,128)}, u32[]{:S(2)}) %copy-start) | copy-done | bytes 5242904
  42.4 0.0 copy-start.1
  42.4 1.0 %copy-done.1 = f32[4,6,4,8,128]{4,3,2,1,0:T(8,128)S(1)} copy-done((f32[4,6,4,8,128]{4,3,2,1,0:T(8,128)S(1)}, f32[4,6,4,8,128]{4,3,2,1,0:T(8,128)}, u32[]{:S(2)}) %copy-start.1) | copy-done | bytes 393240
  43.4 2.0 %shard_map.77 = (f32[16,32,512]{2,1,0:T(8,128)}, f32[16,32,512]{2,1,0:T(8,128)}, f32[16,32,512]{2,1,0:T(8,128)}) custom-call(f32[5,4,16,4,8,128]{5,4,3,2,1,0:T(8,128)S(1)} %copy-done, f32[4,6,4,8,128]{4,3,2,1,0:T(8,128)S(1)} %copy-done.1), custom_call_target="tpu_custom_call" | custom-call | tf_op jit(solution)/shard_map/pallas_call | solution.py:477
Async XLA Ops:
  39.9 2.5 %copy-start = (f32[5,4,16,4,8,128]{5,4,3,2,1,0:T(8,128)S(1)}, f32[5,4,16,4,8,128]{5,4,3,2,1,0:T(8,128)}, u32[]{:S(2)}) copy-start(f32[5,4,16,4,8,128]{5,4,3,2,1,0:T(8,128)} %get-tuple-element.5.V) | copy-start | bytes 15728644
  42.4 1.0 %copy-start.1 = (f32[4,6,4,8,128]{4,3,2,1,0:T(8,128)S(1)}, f32[4,6,4,8,128]{4,3,2,1,0:T(8,128)}, u32[]{:S(2)}) copy-start(f32[4,6,4,8,128]{4,3,2,1,0:T(8,128)} %get-tuple-element.6.ends) | copy-start | bytes 1179652

commit v3 on v2

--- a/solution.py
+++ b/solution.py
@@ -86,10 +86,10 @@
             device_id=(gx + 2 * s - 1, gy), device_id_type=MESH,
         )
 
-    def y_copy(s):
-        return pltpu.make_async_remote_copy(
-            src_ref=ES.at[s], dst_ref=ER.at[1 - s],
-            send_sem=y_send.at[s], recv_sem=y_recv.at[1 - s],
+    def y_copy(s, f):
+        return pltpu.make_async_remote_copy(
+            src_ref=ES.at[s, f], dst_ref=ER.at[1 - s, f],
+            send_sem=y_send.at[s, f], recv_sem=y_recv.at[1 - s, f],
             device_id=(gx, gy + 2 * s - 1), device_id_type=MESH,
         )
 
@@ -118,22 +118,17 @@
         def _():
             wv[(X + 1) * s] = jnp.zeros((ROWS, LANES), jnp.float32)
 
-    for copy in local_copies():
-        copy.wait()
-
     edge = (PAD, PAD + Y - 1)
     outer = (PAD - 1, PAD + Y)
-
-    def pack(f, carry):
+    arriving = local_copies()
+    for f in range(FIELDS):
+        for copy in arriving[f * T:(f + 1) * T]:
+            copy.wait()
         for s in (0, 1):
-            ES[s, f] = F[f, 1:X + 1, :, edge[s]:edge[s] + 1, :]
-        return carry
-
-    lax.fori_loop(0, FIELDS, pack, 0)
-    for s in (0, 1):
-        @pl.when(has_y[s])
-        def _():
-            y_copy(s).start()
+            @pl.when(has_y[s])
+            def _():
+                ES[s, f] = F[f, 1:X + 1, :, edge[s]:edge[s] + 1, :]
+                y_copy(s, f).start()
     for a in (0, 1):
         for b in (0, 1):
             @pl.when(jnp.logical_and(has_x[a], has_y[b]))
@@ -271,18 +266,104 @@
         for k, value in enumerate((f0, f1, f2, fl, fr, v0, v1, v2, l, c)):
             TP[yc, k] = value
 
-    def inner(k, carry):
-        compute_chunk(k)
+    def p_copy(yc):
+        return pltpu.make_async_remote_copy(
+            src_ref=PS.at[yc], dst_ref=PR.at[yc],
+            send_sem=p_send.at[yc], recv_sem=p_recv.at[yc],
+            device_id=(gx + 1, gy), device_id_type=MESH,
+        )
+
+    def s_copy(yc):
+        return pltpu.make_async_remote_copy(
+            src_ref=SS.at[yc], dst_ref=SR.at[yc],
+            send_sem=s_send.at[yc], recv_sem=s_recv.at[yc],
+            device_id=(gx - 1, gy), device_id_type=MESH,
+        )
+
+    @pl.when(gx == 0)
+    def _():
+        PR[...] = jnp.zeros(PR.shape, jnp.float32)
+
+    @pl.when(gx == nx - 1)
+    def _():
+        SR[...] = jnp.zeros(SR.shape, jnp.float32)
+
+    def relate(yc, came, give, near, far):
+        near0, near_own, near_other = near
+        far0, far_own, far_other = far
+        q = came[yc, 3]
+        own = TP[yc, near_own]
+        m = q / (1.0 - own * q)
+        gain = TP[yc, far_own]
+        for k in range(3):
+            p = came[yc, k]
+            give[yc, k] = TP[yc, far0 + k] + gain * (p + m * (TP[yc, near0 + k] + own * p))
+        give[yc, 3] = TP[yc, far_other] + gain * m * TP[yc, near_other]
+
+    def close(yc):
+        t_p, q_p = SR[yc, 3], PS[yc, 3]
+        t_s, q_s = PR[yc, 3], SS[yc, 3]
+        high_inv = 1.0 / (1.0 - t_p * q_p)
+        low_inv = 1.0 / (1.0 - t_s * q_s)
+        for k in range(3):
+            ends_out[yc, k] = (PR[yc, k] + t_s * SS[yc, k]) * low_inv
+            ends_out[yc, 3 + k] = (SR[yc, k] + t_p * PS[yc, k]) * high_inv
+
+    def pass_up(k, carry):
+        @pl.when(has_x[0])
+        def _():
+            p_copy(k).wait_recv()
+        relate(k, PR, PS, (0, 3, 4), (5, 8, 9))
+
+        @pl.when(has_x[1])
+        def _():
+            p_copy(k).start()
         return carry
 
-    if chunks > 2:
-        lax.fori_loop(1, chunks - 1, inner, 0)
+    def pass_down(k, carry):
+        @pl.when(has_x[1])
+        def _():
+            s_copy(k).wait_recv()
+        relate(k, SR, SS, (5, 9, 8), (0, 4, 3))
+
+        @pl.when(has_x[0])
+        def _():
+            s_copy(k).start()
+        return carry
+
+    ends = min(2, chunks)
+
+    def loop_inner(body):
+        if chunks > 2:
+            lax.fori_loop(1, chunks - 1, body, 0)
+
+    def loop_outermost(body):
+        lax.fori_loop(0, ends, lambda k, carry: body(k * (chunks - 1), carry), 0)
+
+    low_half = gx < nx // 2
+
+    def in_order(loop, low_body, high_body):
+        @pl.when(low_half)
+        def _():
+            loop(low_body)
+
+        @pl.when(jnp.logical_not(low_half))
+        def _():
+            loop(high_body)
+
+    def compute_step(yc, carry):
+        compute_chunk(yc)
+        return carry
+
+    loop_inner(compute_step)
+    in_order(loop_inner, pass_up, pass_down)
 
     for s in (0, 1):
         @pl.when(has_y[s])
         def _():
-            y_copy(s).wait_send()
-            y_copy(1 - s).wait_recv()
+            for f in range(FIELDS):
+                y_copy(s, f).wait_send()
+                y_copy(1 - s, f).wait_recv()
 
             def spread(f, carry):
                 F[f, 1:X + 1, :, outer[s]:outer[s] + 1, :] = ER[s, f]
@@ -297,90 +378,10 @@
                 for f in (0, 1):
                     F[f, (X + 1) * a, :, outer[b]:outer[b] + 1, :] = CR[a, b, f]
 
-    ends = min(2, chunks)
-
-    def outermost(k, carry):
-        compute_chunk(k * (chunks - 1))
-        return carry
-
-    lax.fori_loop(0, ends, outermost, 0)
-
-    def p_copy(yc):
-        return pltpu.make_async_remote_copy(
-            src_ref=PS.at[yc], dst_ref=PR.at[yc],
-            send_sem=p_send.at[yc], recv_sem=p_recv.at[yc],
-            device_id=(gx + 1, gy), device_id_type=MESH,
-        )
-
-    def s_copy(yc):
-        return pltpu.make_async_remote_copy(
-            src_ref=SS.at[yc], dst_ref=SR.at[yc],
-            send_sem=s_send.at[yc], recv_sem=s_recv.at[yc],
-            device_id=(gx - 1, gy), device_id_type=MESH,
-        )
-
-    @pl.when(gx == 0)
-    def _():
-        PR[...] = jnp.zeros(PR.shape, jnp.float32)
-
-    @pl.when(gx == nx - 1)
-    def _():
-        SR[...] = jnp.zeros(SR.shape, jnp.float32)
-
-    def relate(yc, came, give, near, far):
-        near0, near_own, near_other = near
-        far0, far_own, far_other = far
-        q = came[yc, 3]
-        own = TP[yc, near_own]
-        m = q / (1.0 - own * q)
-        gain = TP[yc, far_own]
-        for k in range(3):
-            p = came[yc, k]
-            give[yc, k] = TP[yc, far0 + k] + gain * (p + m * (TP[yc, near0 + k] + own * p))
-        give[yc, 3] = TP[yc, far_other] + gain * m * TP[yc, near_other]
-
-    def close(yc):
-        t_p, q_p = SR[yc, 3], PS[yc, 3]
-        t_s, q_s = PR[yc, 3], SS[yc, 3]
-        high_inv = 1.0 / (1.0 - t_p * q_p)
-        low_inv = 1.0 / (1.0 - t_s * q_s)
-        for k in range(3):
-            ends_out[yc, k] = (PR[yc, k] + t_s * SS[yc, k]) * low_inv
-            ends_out[yc, 3 + k] = (SR[yc, k] + t_p * PS[yc, k]) * high_inv
-
-    def pass_up(k, carry):
-        @pl.when(has_x[0])
-        def _():
-            p_copy(k).wait_recv()
-        relate(k, PR, PS, (0, 3, 4), (5, 8, 9))
-
-        @pl.when(has_x[1])
-        def _():
-            p_copy(k).start()
-        return carry
-
-    def pass_down(k, carry):
-        @pl.when(has_x[1])
-        def _():
-            s_copy(k).wait_recv()
-        relate(k, SR, SS, (5, 9, 8), (0, 4, 3))
-
-        @pl.when(has_x[0])
-        def _():
-            s_copy(k).start()
-        return carry
-
-    low_half = gx < nx // 2
-
-    @pl.when(low_half)
-    def _():
-        lax.fori_loop(0, chunks, pass_up, 0)
-        lax.fori_loop(0, chunks, pass_down, 0)
-
-    @pl.when(jnp.logical_not(low_half))
-    def _():
-        lax.fori_loop(0, chunks, pass_down, 0)
-        lax.fori_loop(0, chunks, pass_up, 0)
+    loop_outermost(compute_step)
+    in_order(loop_outermost, pass_up, pass_down)
+    in_order(loop_inner, pass_down, pass_up)
+    in_order(loop_outermost, pass_down, pass_up)
 
     def close_step(yc, carry):
         close(yc)
@@ -441,8 +442,8 @@
     rows, ends = pl.pallas_call(
         functools.partial(kernel, nx, ny),
         out_shape=(
-            jax.ShapeDtypeStruct((5, chunks, X, T, ROWS, LANES), f32),
-            jax.ShapeDtypeStruct((chunks, 6, T, ROWS, LANES), f32),
+            pltpu.VMEM((5, chunks, X, T, ROWS, LANES), f32),
+            pltpu.VMEM((chunks, 6, T, ROWS, LANES), f32),
         ),
         in_specs=[in_hbm] * 5,
         out_specs=(in_vmem,) * 2,
@@ -464,14 +465,14 @@
             pltpu.SMEM((X,), f32),
             dma, dma((FIELDS, T)),
             dma((2, FIELDS)), dma((2, FIELDS)),
-            dma((2,)), dma((2,)),
+            dma((2, FIELDS)), dma((2, FIELDS)),
             dma((2, 2)), dma((2, 2)),
             dma((2,)), dma((2,)),
             dma((chunks,)), dma((chunks,)),
             dma((chunks,)), dma((chunks,)),
         ],
         compiler_params=pltpu.CompilerParams(
-            collective_id=0, has_side_effects=True, vmem_limit_bytes=57 * 1024 * 1024
+            collective_id=0, has_side_effects=True, vmem_limit_bytes=54 * 1024 * 1024
         ),
     )(u_velocity, v_velocity, w_velocity, viscosity, cell_width)
     return pl.pallas_call(

time: 45.5 us -> 38.5 us (0.85)
  Pallas kernels: 41.2 us -> 37.7 us
  local copies, waits for them, and re-layouts: 3.47 us -> 0 us
    pallas_call x1, Pallas kernels: 39.2 us -> 35.7 us  [per_device(): pl.pallas_call(functools.partial(kernel, nx, ny), out_shape=(pltpu.VMEM((...]
    unnamed x4 -> x0, local copies, waits for them, and re-layouts: 3.47 us -> none
where the time goes in v3:
time: 38.5 us; the launch traced here: 38.3 us
  Pallas kernels  37.7 us (98%)
  between operations  0.64 us (2%)
    pallas_call x1, Pallas kernels, per_device(): pl.pallas_call(functools.partial(kernel, nx, ny), out_shape=(pltpu.VMEM((...  35.7 us
    pallas_call x1, Pallas kernels, per_device(): pl.pallas_call(substitute, out_shape=(out, out, out), in_specs=[in_vmem]...  1.96 us

profile of v3, /device:TPU:0, one launch (start us, length us, event | category | flops | bytes accessed | tf_op | source)
XLA Modules:
  0.0 38.3 jit_solution(17938971076331980682)
XLA Ops:
  0.6 35.7 %shard_map.76 = (f32[5,4,16,4,8,128]{5,4,3,2,1,0:T(8,128)S(1)}, f32[4,6,4,8,128]{4,3,2,1,0:T(8,128)S(1)}) custom-call(f32[16,32,512]{2,1,0:T(8,128)} %u_ref.1, f32[16,32,512]{2,1,0:T(8,128)} %v_ref.1, f32[16,32,512]{2,1,0:T(8,128)} %w_ref.1, f32[16,32,512]{2,1,0:T(8,128)} %nu_ref.1, f32[16]{0:T(128)} %width_in.1), custom_call_target="tpu_custom_call" | custom-call | tf_op jit(solution)/shard_map/pallas_call | solution.py:442
  36.3 2.0 %shard_map.77 = (f32[16,32,512]{2,1,0:T(8,128)}, f32[16,32,512]{2,1,0:T(8,128)}, f32[16,32,512]{2,1,0:T(8,128)}) custom-call(f32[5,4,16,4,8,128]{5,4,3,2,1,0:T(8,128)S(1)} %get-tuple-element.5.V, f32[4,6,4,8,128]{4,3,2,1,0:T(8,128)S(1)} %get-tuple-element.6.ends), custom_call_target="tpu_custom_call" | custom-call | tf_op jit(solution)/shard_map/pallas_call | solution.py:478

commit v4 on v3

--- a/solution.py
+++ b/solution.py
@@ -261,7 +261,7 @@
         one = jnp.ones((T, ROWS, LANES), jnp.float32)
         state = (flux_uy(0), flux_uy(1), ld(3, 0) * z_diff(u_low), ld(3, 1) * (u_zn - u_zp), u_zn, u_zp,
                  zero, zero, zero, zero, one, zero, zero, zero, zero, one)
-        state = lax.fori_loop(0, X, row, state)
+        state = lax.fori_loop(0, X, row, state, unroll=8)
         c, v0, v1, v2, l, f0, f1, f2, fl, fr = state[6:]
         for k, value in enumerate((f0, f1, f2, fl, fr, v0, v1, v2, l, c)):
             TP[yc, k] = value
@@ -353,6 +353,18 @@
 
     def compute_step(yc, carry):
         compute_chunk(yc)
+        return carry
+
+    def compute_and_pass(yc, carry):
+        compute_chunk(yc)
+
+        @pl.when(low_half)
+        def _():
+            pass_up(yc, 0)
+
+        @pl.when(jnp.logical_not(low_half))
+        def _():
+            pass_down(yc, 0)
         return carry
 
     loop_inner(compute_step)
@@ -378,8 +390,7 @@
                 for f in (0, 1):
                     F[f, (X + 1) * a, :, outer[b]:outer[b] + 1, :] = CR[a, b, f]
 
-    loop_outermost(compute_step)
-    in_order(loop_outermost, pass_up, pass_down)
+    loop_outermost(compute_and_pass)
     in_order(loop_inner, pass_down, pass_up)
     in_order(loop_outermost, pass_down, pass_up)
 
@@ -419,7 +430,7 @@
                     O[k, i, pl.ds(pl.multiple_of(yc * ROWS, ROWS), ROWS), t * LANES:(t + 1) * LANES] = now[k][t]
             return now
 
-        lax.fori_loop(0, X, row, tuple(ends[yc, 3 + k] for k in range(3)))
+        lax.fori_loop(0, X, row, tuple(ends[yc, 3 + k] for k in range(3)), unroll=4)
         for k in range(3):
             copy(k, yc).start()
         return carry

time: 38.5 us -> 33.5 us (0.87)
  Pallas kernels: 37.7 us -> 32.7 us
    pallas_call x1, Pallas kernels: 35.7 us -> 30.8 us  [per_device(): pl.pallas_call(functools.partial(kernel, nx, ny), out_shape=(pltpu.VMEM((...]
where the time goes in v4:
time: 33.5 us; the launch traced here: 33.3 us
  Pallas kernels  32.7 us (98%)
  between operations  0.64 us (2%)
    pallas_call x1, Pallas kernels, per_device(): pl.pallas_call(functools.partial(kernel, nx, ny), out_shape=(pltpu.VMEM((...  30.8 us
    pallas_call x1, Pallas kernels, per_device(): pl.pallas_call(substitute, out_shape=(out, out, out), in_specs=[in_vmem]...  1.91 us

profile of v4, /device:TPU:0, one launch (start us, length us, event | category | flops | bytes accessed | tf_op | source)
XLA Modules:
  0.0 33.3 jit_solution(17182952183835719330)
XLA Ops:
  0.6 30.8 %shard_map.76 = (f32[5,4,16,4,8,128]{5,4,3,2,1,0:T(8,128)S(1)}, f32[4,6,4,8,128]{4,3,2,1,0:T(8,128)S(1)}) custom-call(f32[16,32,512]{2,1,0:T(8,128)} %u_ref.1, f32[16,32,512]{2,1,0:T(8,128)} %v_ref.1, f32[16,32,512]{2,1,0:T(8,128)} %w_ref.1, f32[16,32,512]{2,1,0:T(8,128)} %nu_ref.1, f32[16]{0:T(128)} %width_in.1), custom_call_target="tpu_custom_call" | custom-call | tf_op jit(solution)/shard_map/pallas_call | solution.py:453
  31.4 1.9 %shard_map.77 = (f32[16,32,512]{2,1,0:T(8,128)}, f32[16,32,512]{2,1,0:T(8,128)}, f32[16,32,512]{2,1,0:T(8,128)}) custom-call(f32[5,4,16,4,8,128]{5,4,3,2,1,0:T(8,128)S(1)} %get-tuple-element.5.V, f32[4,6,4,8,128]{4,3,2,1,0:T(8,128)S(1)} %get-tuple-element.6.ends), custom_call_target="tpu_custom_call" | custom-call | tf_op jit(solution)/shard_map/pallas_call | solution.py:489

commit v5 on v4

--- a/solution.py
+++ b/solution.py
@@ -261,7 +261,7 @@
         one = jnp.ones((T, ROWS, LANES), jnp.float32)
         state = (flux_uy(0), flux_uy(1), ld(3, 0) * z_diff(u_low), ld(3, 1) * (u_zn - u_zp), u_zn, u_zp,
                  zero, zero, zero, zero, one, zero, zero, zero, zero, one)
-        state = lax.fori_loop(0, X, row, state, unroll=8)
+        state = lax.fori_loop(0, X, row, state, unroll=True)
         c, v0, v1, v2, l, f0, f1, f2, fl, fr = state[6:]
         for k, value in enumerate((f0, f1, f2, fl, fr, v0, v1, v2, l, c)):
             TP[yc, k] = value

time: 33.5 us -> 32.8 us (0.979)
  Pallas kernels: 32.7 us -> 32 us
    pallas_call x1, Pallas kernels: 30.8 us -> 30.1 us  [per_device(): pl.pallas_call(functools.partial(kernel, nx, ny), out_shape=(pltpu.VMEM((...]
where the time goes in v5:
time: 32.8 us; the launch traced here: 32.7 us
  Pallas kernels  32 us (98%)
  between operations  0.64 us (2%)
    pallas_call x1, Pallas kernels, per_device(): pl.pallas_call(functools.partial(kernel, nx, ny), out_shape=(pltpu.VMEM((...  30.1 us
    pallas_call x1, Pallas kernels, per_device(): pl.pallas_call(substitute, out_shape=(out, out, out), in_specs=[in_vmem]...  1.91 us

profile of v5, /device:TPU:0, one launch (start us, length us, event | category | flops | bytes accessed | tf_op | source)
XLA Modules:
  0.0 32.7 jit_solution(15189138734402455080)
XLA Ops:
  0.6 30.1 %shard_map.76 = (f32[5,4,16,4,8,128]{5,4,3,2,1,0:T(8,128)S(1)}, f32[4,6,4,8,128]{4,3,2,1,0:T(8,128)S(1)}) custom-call(f32[16,32,512]{2,1,0:T(8,128)} %u_ref.1, f32[16,32,512]{2,1,0:T(8,128)} %v_ref.1, f32[16,32,512]{2,1,0:T(8,128)} %w_ref.1, f32[16,32,512]{2,1,0:T(8,128)} %nu_ref.1, f32[16]{0:T(128)} %width_in.1), custom_call_target="tpu_custom_call" | custom-call | tf_op jit(solution)/shard_map/pallas_call | solution.py:453
  30.8 1.9 %shard_map.77 = (f32[16,32,512]{2,1,0:T(8,128)}, f32[16,32,512]{2,1,0:T(8,128)}, f32[16,32,512]{2,1,0:T(8,128)}) custom-call(f32[5,4,16,4,8,128]{5,4,3,2,1,0:T(8,128)S(1)} %get-tuple-element.5.V, f32[4,6,4,8,128]{4,3,2,1,0:T(8,128)S(1)} %get-tuple-element.6.ends), custom_call_target="tpu_custom_call" | custom-call | tf_op jit(solution)/shard_map/pallas_call | solution.py:489
